TPU v7x, 256 devices: a whole 4x4x8 slice. The times are simulated.
256 devices in a mesh: row: 32 (over x, y, core), col: 8 (over z).
Axes of the slice: x: 4, y: 4, z: 8, core: 2. Of those that a mesh axis runs over, the one named last changes fastest.
Arguments:
- tokens: bfloat16 [512, 8192], P('row', 'col'), may hold values from -6 to 6
- gate_up: bfloat16 [8192, 2, 28672], P('col', None, 'row'), may hold values from -0.0625 to 0.0625
- down: bfloat16 [28672, 8192], P('row', 'col'), may hold values from -0.03125 to 0.03125
- target: bfloat16 [512, 8192], P('row', 'col'), may hold values from -6 to 6
Outputs:
- output: bfloat16 [512, 8192], P('row', 'col')
- grad_tokens: bfloat16 [512, 8192], P('row', 'col')
- grad_gate_up: bfloat16 [8192, 2, 28672], P('col', None, 'row')
- grad_down: bfloat16 [28672, 8192], P('row', 'col')
All inputs are finite; a program needn't handle non-finite values.
Results may differ from a plain program's by a relative error of at most 0.04.
Values may be sent and summed in bfloat16 or wider, within the bound.
No kernel may reach another device: no remote copies, remote signals or barrier semaphores. Data moves between devices by JAX's collectives and lax.ppermute only.
A program may use at most 64 MiB of HBM per device.

v0:
```python
import jax
import jax.numpy as jnp
from jax import lax
from jax.sharding import PartitionSpec as P


def gather_rows(value):
    return lax.all_gather(value, "row", axis=0, tiled=True)


def gather_cols(value):
    return lax.all_gather(value, "col", axis=0, tiled=True)


def scatter_cols(value):
    return lax.psum_scatter(
        value.astype(jnp.bfloat16), "col", scatter_dimension=0, tiled=True
    ).astype(jnp.float32)


def scatter_rows(value):
    return lax.psum_scatter(
        value.astype(jnp.bfloat16), "row", scatter_dimension=0, tiled=True
    ).astype(jnp.float32)


def row_sum(term_fn, total_rows):
    return scatter_rows(term_fn(0, total_rows))


def swiglu_grad(grad_hidden, gate, up):
    sigma = jax.nn.sigmoid(gate)
    grad_gate = grad_hidden * up * sigma * (1.0 + gate * (1.0 - sigma))
    grad_up = grad_hidden * gate * sigma
    return jnp.stack([grad_gate, grad_up], axis=1).astype(jnp.bfloat16)


def per_device(tokens, gate_up, down, target):
    all_tokens = gather_rows(tokens)
    total_rows = all_tokens.shape[0]
    partial_value = jnp.einsum(
        "td,dgf->tgf", all_tokens, gate_up, preferred_element_type=jnp.float32
    )
    projected = scatter_cols(partial_value)
    gate = projected[:, 0]
    up = projected[:, 1]
    hidden = (jax.nn.silu(gate) * up).astype(jnp.bfloat16)
    all_hidden = gather_cols(hidden)

    def mixed_term(start, count):
        return jnp.dot(all_hidden, down, preferred_element_type=jnp.float32)

    mixed = row_sum(mixed_term, total_rows)
    output = (tokens.astype(jnp.float32) + mixed).astype(jnp.bfloat16)
    delta = (output.astype(jnp.float32) - target.astype(jnp.float32)).astype(jnp.bfloat16)
    all_delta = gather_rows(delta)
    hidden_part = jnp.einsum("td,fd->tf", all_delta, down, preferred_element_type=jnp.float32)
    grad_down = jnp.einsum(
        "tf,td->fd", all_hidden, all_delta, preferred_element_type=jnp.float32
    ).astype(jnp.bfloat16)
    grad_hidden = scatter_cols(hidden_part)
    all_grad = gather_cols(swiglu_grad(grad_hidden, gate, up))
    grad_gate_up = jnp.einsum(
        "td,tgf->dgf", all_tokens, all_grad, preferred_element_type=jnp.float32
    ).astype(jnp.bfloat16)

    def inner_term(start, count):
        return jnp.einsum("tgf,dgf->td", all_grad, gate_up, preferred_element_type=jnp.float32)

    grad_inner = row_sum(inner_term, total_rows)
    grad_tokens = (delta.astype(jnp.float32) + grad_inner).astype(jnp.bfloat16)
    return (output, grad_tokens, grad_gate_up, grad_down)


def solution(mesh):
    in_specs = (P("row", "col"), P("col", None, "row"), P("row", "col"), P("row", "col"))
    out_specs = (P("row", "col"), P("row", "col"), P("col", None, "row"), P("row", "col"))
    return jax.shard_map(
        per_device, mesh=mesh, in_specs=in_specs, out_specs=out_specs, check_vma=False
    )
```

profile of v0, /device:TPU:2, one launch (start us, length us, event | category | flops | bytes accessed | tf_op | source)
XLA Modules:
  0.0 452.4 jit_solution(11210774648093839620)
XLA Ops:
  7.2 0.7 all-gather.4.cloned.1.call-update
  8.0 53.1 %all-gather.4.cloned.1.call-done = bf16[512,1024]{1,0:T(8,128)(2,1)} async-done(((bf16[16,1024]{1,0:T(8,128)(2,1)}), bf16[512,1024]{1,0:T(8,128)(2,1)}) %all-gather.4.cloned.1.call-update) | async-done | bytes 1048592 | tf_op jit(solution)/shard_map/all_gather | solution.py:8
  61.0 5.7 %fusion.4 = bf16[512,2,896]{2,0,1:T(8,128)(2,1)} fusion(bf16[1024,2,896]{2,1,0:T(2,128)(2,1)} %param.5, bf16[512,1024]{1,0:T(8,128)(2,1)} %all-gather.4.cloned.1.call-done), kind=kOutput, calls=%fused_computation.6 | convolution fusion | flops 1879965696 | bytes 6553600 | tf_op jit(solution)/shard_map/td,dgf->tgf/dot_general | solution.py:41
  66.8 41.1 %reduce-scatter.5.cloned.1.call-done = bf16[64,2,896]{2,0,1:T(8,128)(2,1)} async-done(((bf16[512,2,896]{2,0,1:T(8,128)(2,1)}), bf16[64,2,896]{2,0,1:T(8,128)(2,1)}) %reduce-scatter.5.cloned.1.call-update) | async-done | bytes 229392 | tf_op jit(solution)/shard_map/reduce_scatter | solution.py:16
  107.8 1.0 convert_element_type.60
  108.8 0.1 multiply_convert_fusion
  108.9 26.3 %all_gather.13 = bf16[512,896]{1,0:T(8,128)(2,1)S(1)} all-gather(bf16[64,896]{1,0:T(8,128)(2,1)S(1)} %multiply_convert_fusion), channel_id=1, replica_groups=mesh['row'=32,'col'=8] {'col'}, dimensions={0}, use_global_device_ids=true | all-gather | bytes 1032192 | tf_op jit(solution)/shard_map/all_gather | solution.py:12
  135.2 2.2 convolution_convert_fusion.1
  137.5 0.0 all-gather.6.cloned.1.call-start
  137.5 84.0 %reduce-scatter.7.cloned.1.call-done = bf16[16,1024]{1,0:T(8,128)(2,1)} async-done(((bf16[512,1024]{1,0:T(8,128)(2,1)}), bf16[16,1024]{1,0:T(8,128)(2,1)}) %reduce-scatter.7.cloned.1.call-update) | async-done | bytes 32784 | tf_op jit(solution)/shard_map/reduce_scatter | solution.py:22
  221.5 1.4 subtract_convert_fusion
  222.9 0.0 reduce-scatter.9.cloned.1.call-start
  223.0 49.1 %all-gather.6.cloned.1.call-done = bf16[512,1024]{1,0:T(8,128)(2,1)} async-done(((bf16[16,1024]{1,0:T(8,128)(2,1)}), bf16[512,1024]{1,0:T(8,128)(2,1)}) %all-gather.6.cloned.1.call-update) | async-done | bytes 1048592 | tf_op jit(solution)/shard_map/all_gather | solution.py:8
  272.0 3.4 convolution_convert_fusion.2
  275.5 38.0 %reduce-scatter.9.cloned.1.call-done = bf16[64,896]{1,0:T(8,128)(2,1)} async-done(((bf16[512,896]{1,0:T(8,128)(2,1)}), bf16[64,896]{1,0:T(8,128)(2,1)}) %reduce-scatter.9.cloned.1.call-update) | async-done | bytes 114704 | tf_op jit(solution)/shard_map/reduce_scatter | solution.py:16
  313.5 1.0 fusion.17
  314.5 0.7 pad_maximum_fusion
  315.3 39.7 %all-gather.8.cloned.1.call-done = bf16[512,2,896]{2,0,1:T(8,128)(2,1)} async-done(((bf16[64,2,896]{2,0,1:T(8,128)(2,1)}), bf16[512,2,896]{2,0,1:T(8,128)(2,1)}) %all-gather.8.cloned.1.call-update) | async-done | bytes 1835024 | tf_op jit(solution)/shard_map/all_gather | solution.py:12
  355.0 5.7 %bitcast_convert_fusion = bf16[512,1024]{1,0:T(8,128)(2,1)} fusion(bf16[512,2,896]{2,0,1:T(8,128)(2,1)} %all-gather.8.cloned.1.call-done, bf16[1024,2,896]{2,1,0:T(2,128)(2,1)} %param.5), kind=kOutput, calls=%fused_computation.5 | convolution fusion | flops 1879572480 | bytes 6553600 | tf_op jit(solution)/shard_map/tgf,dgf->td/dot_general | solution.py:68
  360.7 3.8 convolution_convert_fusion
  364.4 3.9 convert_bitcast_fusion
  368.3 10.0 %copy.10 = bf16[1024,2,896]{2,1,0:T(2,128)(2,1)} copy(bf16[1024,2,896]{0,2,1:T(8,128)(2,1)} %convert_bitcast_fusion) | data formatting | bytes 7340032
  378.3 65.9 %reduce-scatter.11.cloned.1.call-done = bf16[16,1024]{1,0:T(8,128)(2,1)} async-done(((bf16[512,1024]{1,0:T(8,128)(2,1)}), bf16[16,1024]{1,0:T(8,128)(2,1)}) %reduce-scatter.11.cloned.1.call-update) | async-done | bytes 32784 | tf_op jit(solution)/shard_map/reduce_scatter | solution.py:22
  444.2 1.4 add_convert_fusion
  (23 shorter events, 0.3 us)
Async XLA Ops:
  7.2 128.0 %copy-start = (bf16[896,1024]{1,0:T(8,128)(2,1)S(1)}, bf16[896,1024]{1,0:T(8,128)(2,1)}, u32[]{:S(2)}) copy-start(bf16[896,1024]{1,0:T(8,128)(2,1)} %param.6) | copy-start | bytes 5505028
  7.2 53.8 %all-gather.4.cloned.1.call-start = ((), (), s32[]{:S(2)}) async-start(), calls=%async_computation.4 | async-start | bytes 1081344 | tf_op jit(solution)/shard_map/all_gather | solution.py:8
  7.9 99.9 %reduce-scatter.5.cloned.1.call-start = ((), (), s32[]{:S(2)}) async-start(), calls=%async_computation.5 | async-start | bytes 2064384 | tf_op jit(solution)/shard_map/reduce_scatter | solution.py:16
  66.7 154.8 %reduce-scatter.7.cloned.1.call-start = ((), (), s32[]{:S(2)}) async-start(), calls=%async_computation.6 | async-start | bytes 1081344 | tf_op jit(solution)/shard_map/reduce_scatter | solution.py:22
  135.2 86.3 %copy-start.2 = (bf16[16,1024]{1,0:T(8,128)(2,1)S(1)}, bf16[16,1024]{1,0:T(8,128)(2,1)}, u32[]{:S(2)}) copy-start(bf16[16,1024]{1,0:T(8,128)(2,1)} %param.4) | copy-start | bytes 98308
  135.2 86.3 %copy-start.3 = (bf16[16,1024]{1,0:T(8,128)(2,1)S(1)}, bf16[16,1024]{1,0:T(8,128)(2,1)}, u32[]{:S(2)}) copy-start(bf16[16,1024]{1,0:T(8,128)(2,1)} %param.7) | copy-start | bytes 98308
  137.5 134.6 %all-gather.6.cloned.1.call-start = ((), (), s32[]{:S(2)}) async-start(), calls=%async_computation.7 | async-start | bytes 1081344 | tf_op jit(solution)/shard_map/all_gather | solution.py:8
  222.9 90.6 %reduce-scatter.9.cloned.1.call-start = ((), (), s32[]{:S(2)}) async-start(), calls=%async_computation.8 | async-start | bytes 1032192 | tf_op jit(solution)/shard_map/reduce_scatter | solution.py:16
  275.5 79.5 %all-gather.8.cloned.1.call-start = ((), (), s32[]{:S(2)}) async-start(), calls=%async_computation.9 | async-start | bytes 2064384 | tf_op jit(solution)/shard_map/all_gather | solution.py:12
  315.2 129.0 %reduce-scatter.11.cloned.1.call-start = ((), (), s32[]{:S(2)}) async-start(), calls=%async_computation.10 | async-start | bytes 1081344 | tf_op jit(solution)/shard_map/reduce_scatter | solution.py:22
  360.7 3.8 copy-start.4
  360.7 3.8 copy-start.5
  368.3 75.9 %copy-start.1 = (bf16[16,1024]{1,0:T(8,128)(2,1)S(1)}, bf16[16,1024]{1,0:T(8,128)(2,1)}, u32[]{:S(2)}) copy-start(bf16[16,1024]{1,0:T(8,128)(2,1)} %get-tuple-element.8) | copy-start | bytes 98308
Sparse Core Ops, SparseCore 0:
  10.6 50.4 all-gather.3
  66.8 40.9 reduce-scatter.4
  137.6 83.8 reduce-scatter.6
  224.8 47.1 all-gather.5
  275.6 37.8 reduce-scatter.8
  315.7 39.1 all-gather.7
  360.8 83.3 reduce-scatter.10
where the time goes:
time: 453 us; the launch traced here: 452 us
  waiting for transfers between devices  371 us (82%)
  blocking collectives  26.3 us (6%)
  matrix products  24.6 us (5%)
  between operations  14.2 us (3%)
  local copies, waits for them, and re-layouts  10 us (2%)
  other arithmetic  5.54 us (1%)
    reduce_scatter x2, waiting for transfers between devices, scatter_rows(): lax.psum_scatter(value.astype(jnp.bfloat16), 'row', scatter_dimension=0,...  150 us
    all_gather x2, waiting for transfers between devices, gather_rows(): return lax.all_gather(value, 'row', axis=0, tiled=True)  102 us
    reduce_scatter x2, waiting for transfers between devices, scatter_cols(): lax.psum_scatter(value.astype(jnp.bfloat16), 'col', scatter_dimension=0,...  79 us
    all_gather x1, waiting for transfers between devices, gather_cols(): return lax.all_gather(value, 'col', axis=0, tiled=True)  39.7 us
    all_gather x1, blocking collectives, gather_cols(): return lax.all_gather(value, 'col', axis=0, tiled=True)  26.3 us
    unnamed x13, local copies, waits for them, and re-layouts  10 us
  transfers between devices with their start and end apart: 7, of which 7 were waited for; matrix products, arithmetic and copies ran while one was open for 4% of the time, Pallas kernels for 0%

commit v1 on v0

--- a/solution.py
+++ b/solution.py
@@ -5,7 +5,9 @@
 
 
 def gather_rows(value):
-    return lax.all_gather(value, "row", axis=0, tiled=True)
+    return jnp.concatenate(
+        lax.all_to_all(jnp.stack([value] * lax.axis_size("row")), "row", 0, 0), axis=0
+    )
 
 
 def gather_cols(value):

time: 453 us -> 396 us (0.87)
  waiting for transfers between devices: 371 us -> 271 us
  blocking collectives: 26.3 us -> 68.1 us
    all_gather x2 -> x0, waiting for transfers between devices: 102 us -> none  [gather_rows(): return lax.all_gather(value, 'row', axis=0, tiled=True)]
    all_to_all x0 -> x2, blocking collectives: none -> 41.9 us  [gather_rows(): lax.all_to_all(jnp.stack([value] * lax.axis_size('row')), 'row', 0, 0)]
  transfers between devices with their start and end apart: 7 -> 5, of which waited for: 7 -> 5; matrix products, arithmetic and copies ran while one was open for 4% -> 5% of each run, Pallas kernels for 0% -> 0%
where the time goes in v1:
time: 396 us; the launch traced here: 395 us
  waiting for transfers between devices  271 us (68%)
  blocking collectives  68.1 us (17%)
  matrix products  23.4 us (6%)
  between operations  13.8 us (3%)
  local copies, waits for them, and re-layouts  13 us (3%)
  other arithmetic  5.54 us (1%)
    reduce_scatter x2, waiting for transfers between devices, scatter_rows(): lax.psum_scatter(value.astype(jnp.bfloat16), 'row', scatter_dimension=0,...  150 us
    reduce_scatter x2, waiting for transfers between devices, scatter_cols(): lax.psum_scatter(value.astype(jnp.bfloat16), 'col', scatter_dimension=0,...  81.7 us
    all_to_all x2, blocking collectives, gather_rows(): lax.all_to_all(jnp.stack([value] * lax.axis_size('row')), 'row', 0, 0)  41.9 us
    all_gather x1, waiting for transfers between devices, gather_cols(): return lax.all_gather(value, 'col', axis=0, tiled=True)  39.6 us
    all_gather x1, blocking collectives, gather_cols(): return lax.all_gather(value, 'col', axis=0, tiled=True)  26.2 us
    unnamed x13, local copies, waits for them, and re-layouts  11.9 us
  transfers between devices with their start and end apart: 5, of which 5 were waited for; matrix products, arithmetic and copies ran while one was open for 5% of the time, Pallas kernels for 0%

profile of v1, /device:TPU:2, one launch (start us, length us, event | category | flops | bytes accessed | tf_op | source)
XLA Modules:
  0.0 395.4 jit_solution(12888975152312111725)
XLA Ops:
  7.2 1.0 stack.13
  8.2 21.9 %all_to_all.10 = bf16[32,16,1024]{2,1,0:T(8,128)(2,1)S(1)} all-to-all(bf16[32,16,1024]{2,1,0:T(8,128)(2,1)S(1)} %stack.13), channel_id=1, replica_groups=mesh['row'=32,'col'=8] {'row'}, dimensions={0} | all-to-all | bytes 2097152 | tf_op jit(solution)/shard_map/all_to_all | solution.py:9
  30.1 5.3 %fusion.4 = bf16[512,2,896]{2,0,1:T(8,128)(2,1)} fusion(bf16[512,1024,1]{1,0,2:T(8,128)(2,1)S(1)} %bitcast.42, bf16[1024,2,896]{2,1,0:T(2,128)(2,1)} %param.5), kind=kOutput, calls=%fused_computation.6 | convolution fusion | flops 1879965696 | bytes 6553600 | tf_op jit(solution)/shard_map/td,dgf->tgf/dot_general | solution.py:43
  35.5 43.1 %reduce-scatter.5.cloned.1.call-done = bf16[64,2,896]{2,0,1:T(8,128)(2,1)} async-done(((bf16[512,2,896]{2,0,1:T(8,128)(2,1)}), bf16[64,2,896]{2,0,1:T(8,128)(2,1)}) %reduce-scatter.5.cloned.1.call-update) | async-done | bytes 229392 | tf_op jit(solution)/shard_map/reduce_scatter | solution.py:18
  78.6 1.0 convert_element_type.60
  79.6 26.2 %all_gather.6 = bf16[512,896]{1,0:T(8,128)(2,1)S(1)} all-gather(bf16[64,896]{1,0:T(8,128)(2,1)S(1)} %multiply_convert_fusion), channel_id=1, replica_groups=mesh['row'=32,'col'=8] {'col'}, dimensions={0}, use_global_device_ids=true | all-gather | bytes 1032192 | tf_op jit(solution)/shard_map/all_gather | solution.py:14
  105.8 0.9 copy-done.2
  106.8 2.3 convolution_convert_fusion.1
  109.1 84.2 %reduce-scatter.7.cloned.1.call-done = bf16[16,1024]{1,0:T(8,128)(2,1)} async-done(((bf16[512,1024]{1,0:T(8,128)(2,1)}), bf16[16,1024]{1,0:T(8,128)(2,1)}) %reduce-scatter.7.cloned.1.call-update) | async-done | bytes 32784 | tf_op jit(solution)/shard_map/reduce_scatter | solution.py:24
  193.3 1.4 subtract_convert_fusion
  194.7 0.1 stack.14
  194.8 20.1 %all_to_all.11 = bf16[32,16,1024]{2,1,0:T(8,128)(2,1)S(1)} all-to-all(bf16[32,16,1024]{2,1,0:T(8,128)(2,1)S(1)} %stack.14), channel_id=1, replica_groups=mesh['row'=32,'col'=8] {'row'}, dimensions={0} | all-to-all | bytes 2097152 | tf_op jit(solution)/shard_map/all_to_all | solution.py:9
  214.9 1.0 copy-done.1
  215.9 2.2 convolution_convert_fusion.2
  218.2 38.6 %reduce-scatter.9.cloned.1.call-done = bf16[64,896]{1,0:T(8,128)(2,1)} async-done(((bf16[512,896]{1,0:T(8,128)(2,1)}), bf16[64,896]{1,0:T(8,128)(2,1)}) %reduce-scatter.9.cloned.1.call-update) | async-done | bytes 114704 | tf_op jit(solution)/shard_map/reduce_scatter | solution.py:18
  256.8 1.0 fusion.15
  257.8 0.7 pad_maximum_fusion
  258.6 39.6 %all-gather.2.cloned.1.call-done = bf16[512,2,896]{2,0,1:T(8,128)(2,1)} async-done(((bf16[64,2,896]{2,0,1:T(8,128)(2,1)}), bf16[512,2,896]{2,0,1:T(8,128)(2,1)}) %all-gather.2.cloned.1.call-update) | async-done | bytes 1835024 | tf_op jit(solution)/shard_map/all_gather | solution.py:14
  298.2 5.7 %bitcast_convert_fusion = bf16[512,1024]{1,0:T(8,128)(2,1)} fusion(bf16[512,2,896]{2,0,1:T(8,128)(2,1)} %all-gather.2.cloned.1.call-done, bf16[1024,2,896]{2,1,0:T(2,128)(2,1)} %param.5), kind=kOutput, calls=%fused_computation.5 | convolution fusion | flops 1879572480 | bytes 6553600 | tf_op jit(solution)/shard_map/tgf,dgf->td/dot_general | solution.py:70
  303.9 4.0 %convolution_convert_fusion = bf16[896,1024]{1,0:T(8,128)(2,1)} fusion(bf16[512,896]{1,0:T(8,128)(2,1)} %copy-done.2, bf16[512,1024]{1,0:T(8,128)(2,1)} %bitcast.45), kind=kOutput, calls=%fused_computation.7 | convolution fusion | flops 940441600 | bytes 3801088 | tf_op jit(solution)/shard_map/tf,td->fd/dot_general | solution.py:60
  307.9 3.9 convert_bitcast_fusion
  311.9 10.0 %copy.10 = bf16[1024,2,896]{2,1,0:T(2,128)(2,1)} copy(bf16[1024,2,896]{0,2,1:T(8,128)(2,1)} %convert_bitcast_fusion) | data formatting | bytes 7340032
  321.8 65.7 %reduce-scatter.11.cloned.1.call-done = bf16[16,1024]{1,0:T(8,128)(2,1)} async-done(((bf16[512,1024]{1,0:T(8,128)(2,1)}), bf16[16,1024]{1,0:T(8,128)(2,1)}) %reduce-scatter.11.cloned.1.call-update) | async-done | bytes 32784 | tf_op jit(solution)/shard_map/reduce_scatter | solution.py:24
  387.5 1.4 add_convert_fusion
  (21 shorter events, 0.4 us)
Async XLA Ops:
  7.2 99.6 %copy-start = (bf16[896,1024]{1,0:T(8,128)(2,1)S(1)}, bf16[896,1024]{1,0:T(8,128)(2,1)}, u32[]{:S(2)}) copy-start(bf16[896,1024]{1,0:T(8,128)(2,1)} %param.6) | copy-start | bytes 5505028
  7.2 71.4 %reduce-scatter.5.cloned.1.call-start = ((), (), s32[]{:S(2)}) async-start(), calls=%async_computation.6 | async-start | bytes 2064384 | tf_op jit(solution)/shard_map/reduce_scatter | solution.py:18
  35.5 157.9 %reduce-scatter.7.cloned.1.call-start = ((), (), s32[]{:S(2)}) async-start(), calls=%async_computation.7 | async-start | bytes 1081344 | tf_op jit(solution)/shard_map/reduce_scatter | solution.py:24
  105.8 0.9 copy-start.2
  106.8 86.5 %copy-start.3 = (bf16[16,1024]{1,0:T(8,128)(2,1)S(1)}, bf16[16,1024]{1,0:T(8,128)(2,1)}, u32[]{:S(2)}) copy-start(bf16[16,1024]{1,0:T(8,128)(2,1)} %param.4) | copy-start | bytes 98308
  106.8 86.5 %copy-start.4 = (bf16[16,1024]{1,0:T(8,128)(2,1)S(1)}, bf16[16,1024]{1,0:T(8,128)(2,1)}, u32[]{:S(2)}) copy-start(bf16[16,1024]{1,0:T(8,128)(2,1)} %param.7) | copy-start | bytes 98308
  109.1 147.7 %reduce-scatter.9.cloned.1.call-start = ((), (), s32[]{:S(2)}) async-start(), calls=%async_computation.8 | async-start | bytes 1032192 | tf_op jit(solution)/shard_map/reduce_scatter | solution.py:18
  214.9 1.0 copy-start.1
  218.1 80.1 %all-gather.2.cloned.1.call-start = ((), (), s32[]{:S(2)}) async-start(), calls=%async_computation.9 | async-start | bytes 2064384 | tf_op jit(solution)/shard_map/all_gather | solution.py:14
  258.5 129.0 %reduce-scatter.11.cloned.1.call-start = ((), (), s32[]{:S(2)}) async-start(), calls=%async_computation.10 | async-start | bytes 1081344 | tf_op jit(solution)/shard_map/reduce_scatter | solution.py:24
  303.9 4.0 %copy-start.5 = (bf16[512,2,896]{2,0,1:T(8,128)(2,1)S(1)}, bf16[512,2,896]{2,0,1:T(8,128)(2,1)}, u32[]{:S(2)}) copy-start(bf16[512,2,896]{2,0,1:T(8,128)(2,1)} %all-gather.2.cloned.1.call-done) | copy-start | bytes 5505028
Sparse Core Ops, SparseCore 0:
  35.6 42.9 reduce-scatter.4
  109.2 84.0 reduce-scatter.6
  218.2 38.4 reduce-scatter.8
  259.0 39.1 all-gather.1
  304.0 83.3 reduce-scatter.10
